TPU v7x, 32 devices: a whole 2x2x4 slice. The times are simulated.
32 devices in a mesh: beam: 2 (over y), freq: 8 (over z, x), tm: 2 (over core).
Axes of the slice: x: 2, y: 2, z: 4, core: 2. Of those that a mesh axis runs over, the one named last changes fastest.
Arguments:
- intensity: float32 [128, 8192], P(('beam', 'freq'), 'tm'), parts along dimension 0, may hold values from -6 to 6
- channel_shift: int32 [64, 2], replicated, may hold values from 0 to 15, as said below
- section_shift: int32 [6, 128], replicated, may hold values from 0 to 96, as said below
- filter_bank: float32 [8, 128], replicated, may hold values from -0.5 to 0.5
Outputs:
- power_map: float32 [256, 8, 8], P(('beam', 'freq'), None, 'tm'), parts along dimension 0
There are 2 independent parts, one for each index of `beam`. A program takes and returns all parts, laid end to end along the dimension named above; an argument that names none is the same for every part. Nothing has to cross between parts.
Inputs may be any that keep to these rules, and one draw needn't show every extreme that they name: `channel_shift`: every entry is at most 15, and some entry equals 15. `section_shift`: every entry of row s lies between 0 and 3 * 2^s, and some entry of each row s equals 3 * 2^s.
All inputs are finite; a program needn't handle non-finite values.
Results may differ from a plain program's by a relative error of at most 0.0003.
Values sent between devices are 32-bit elements; how exact they have to be, the bound alone decides.
A program may use at most 64 MiB of HBM per device.

v0:
```python
import jax
import jax.numpy as jnp
from jax import lax
from jax.sharding import PartitionSpec as P

SHIFT_UNIT = 3
CHAN_MAX = 15
BLOCK = 1024


def from_behind(block, axis, distance):
    devices = range(lax.axis_size(axis))
    route = [(i - distance, i) for i in devices if i - distance in devices]
    return lax.ppermute(block, axis, route)


def from_partner(array, axis, distance):
    return lax.ppermute(array, axis, [(i, i ^ 1 << distance) for i in range(lax.axis_size(axis))])


def shifted_rows(row_block, shifts, length):
    extra = row_block.shape[1] - length
    bit_count = max(extra, 0).bit_length()
    target = length + 2**bit_count - 1
    current = row_block
    if target > row_block.shape[1]:
        current = jnp.concatenate(
            [
                row_block,
                jnp.zeros((row_block.shape[0], target - row_block.shape[1]), row_block.dtype),
            ],
            axis=1,
        )
    for bit_index in range(bit_count - 1, -1, -1):
        step = 2**bit_index
        chosen = jnp.bitwise_and(jnp.right_shift(shifts, bit_index), 1)[:, None] == 1
        current = jnp.where(chosen, current[:, step:], current[:, : current.shape[1] - step])
    return current


def merge_bands(lower_band, upper_ext, shift_table, out_len):
    doubled_low = jnp.concatenate([lower_band, lower_band], axis=1)[:, :, :out_len]
    doubled_up = jnp.concatenate([upper_ext, upper_ext], axis=1)
    shifted = shifted_rows(
        doubled_up.reshape(-1, doubled_up.shape[2]), shift_table.reshape(-1), out_len
    )
    return doubled_low + shifted.reshape(doubled_low.shape)


def toeplitz_pair(filter_bank):
    tap_count = filter_bank.shape[1]
    lag_index = jnp.arange(tap_count)[:, None] - jnp.arange(tap_count)[None, :]
    toep_top = jnp.where(
        lag_index >= 0, jnp.take(filter_bank, jnp.clip(lag_index, 0, tap_count - 1), axis=1), 0.0
    )
    lag_later = lag_index + tap_count
    toep_low = jnp.where(
        lag_later < tap_count,
        jnp.take(filter_bank, jnp.clip(lag_later, 0, tap_count - 1), axis=1),
        0.0,
    )
    return (toep_top, toep_low)


def body(intensity, channel_shift, section_shift, filter_bank):
    chan_dev, samples = intensity.shape
    n_freq = lax.axis_size("freq")
    local_levels = chan_dev.bit_length() - 1
    freq_levels = n_freq.bit_length() - 1
    trials_each = channel_shift.shape[1]
    row_count = trials_each * chan_dev
    channels = chan_dev * n_freq
    freq_place = lax.axis_index("freq")
    own_section = lax.dynamic_slice_in_dim(section_shift, freq_place * row_count, row_count, 1)
    local_margin = SHIFT_UNIT * (2**local_levels - 1)
    margin = CHAN_MAX + local_margin
    rim_cols = from_behind(intensity[:, :margin], "tm", -1)
    extended = jnp.concatenate([intensity, rim_cols], axis=1)
    own_chan_shift = lax.dynamic_slice_in_dim(channel_shift, freq_place * chan_dev, chan_dev, 0)
    length = samples + margin - CHAN_MAX
    tree_rows = shifted_rows(
        jnp.repeat(extended, trials_each, axis=0), own_chan_shift.reshape(-1), length
    )
    tree_rows = tree_rows.reshape(chan_dev, trials_each, length)
    for section_index in range(local_levels):
        max_shift = SHIFT_UNIT * 2**section_index
        band_count, band_rows, span_len = tree_rows.shape
        lower_band = tree_rows[0::2]
        upper_band = tree_rows[1::2]
        out_len = span_len - max_shift
        upper_ext = upper_band
        shift_table = own_section[section_index].reshape(band_count // 2, 2 * band_rows)
        tree_rows = merge_bands(lower_band, upper_ext, shift_table, out_len)
    own_rows = tree_rows.reshape(row_count, samples)
    first_cross = 0
    for section_index in range(first_cross, freq_levels):
        max_shift = SHIFT_UNIT * 2 ** (local_levels + section_index)
        shift_table = own_section[local_levels + section_index]
        upper_bit = jnp.bitwise_and(jnp.right_shift(freq_place, section_index), 1)
        is_upper = upper_bit == 1
        sent_rows = own_rows
        partner_rows = from_partner(sent_rows, "freq", section_index)
        lower_band = jnp.where(is_upper, partner_rows, sent_rows)
        upper_band = jnp.where(is_upper, sent_rows, partner_rows)
        upper_rim = from_behind(upper_band[:, :max_shift], "tm", -1)
        upper_ext = jnp.concatenate([upper_band, upper_rim], axis=1)
        own_rows = lower_band + shifted_rows(upper_ext, shift_table, samples)
    tap_count = filter_bank.shape[1]
    filters = filter_bank.shape[0]
    tail_rows = from_behind(own_rows[:, : tap_count - 1], "tm", -1)
    padded = jnp.concatenate(
        [own_rows, tail_rows, jnp.zeros((row_count, 1), own_rows.dtype)], axis=1
    )
    first_half = padded[:, :samples].reshape(-1, tap_count)
    second_half = padded[:, tap_count:].reshape(-1, tap_count)
    toep_top, toep_low = toeplitz_pair(filter_bank)
    outputs = []
    for filter_index in range(filters):
        series = jnp.dot(
            first_half,
            toep_top[filter_index],
            precision=lax.Precision.HIGHEST,
            preferred_element_type=jnp.float32,
        )
        series = series + jnp.dot(
            second_half,
            toep_low[filter_index],
            precision=lax.Precision.HIGHEST,
            preferred_element_type=jnp.float32,
        )
        energy = jnp.sum((series * series).reshape(row_count, samples // BLOCK, BLOCK), axis=2)
        outputs.append(energy)
    return jnp.stack(outputs, axis=1) / (BLOCK * channels)


def solution(mesh):
    in_specs = (P(("beam", "freq"), "tm"), P(), P(), P())
    out_specs = P(("beam", "freq"), None, "tm")
    return jax.shard_map(body, mesh=mesh, in_specs=in_specs, out_specs=out_specs, check_vma=False)
```

profile of v0, /device:TPU:0, one launch (start us, length us, event | category | flops | bytes accessed | tf_op | source)
XLA Modules:
  0.0 171.4 jit_solution(15521919331860812971)
XLA Ops:
  0.0 0.7 slice.299
  0.7 1.3 collective-permute-start
  2.1 0.8 and_compare_fusion.3
  3.8 0.9 pad_maximum_fusion.7
  7.6 3.0 %collective-permute-start.1 = (f32[16,4096]{1,0:T(8,128)S(1)}, f32[16,4096]{1,0:T(8,128)S(1)}, u32[]{:S(2)}, u32[]{:S(2)}) collective-permute-start(f32[16,4096]{1,0:T(8,128)S(1)} %fusion.19), channel_id=1, source_target_pairs={{0,2},{2,0},{4,6},{6,4},{8,10},{10,8},{12,14},{14,12},{1,3},{3,1},... | collective-permute-start | bytes 786440 | tf_op jit(solution)/shard_map/ppermute | solution.py:18
  10.6 6.8 %collective-permute-done.1 = f32[16,4096]{1,0:T(8,128)S(1)} collective-permute-done((f32[16,4096]{1,0:T(8,128)S(1)}, f32[16,4096]{1,0:T(8,128)S(1)}, u32[]{:S(2)}, u32[]{:S(2)}) %collective-permute-start.1) | collective-permute-done | bytes 262176 | tf_op jit(solution)/shard_map/ppermute | solution.py:18
  17.5 1.3 collective-permute-start.2
  18.8 1.8 %collective-permute-done.2 = f32[16,24]{1,0:T(8,128)S(1)} collective-permute-done((f32[16,24]{1,0:T(8,128)S(1)}, f32[16,24]{1,0:T(8,128)S(1)}, u32[]{:S(2)}, u32[]{:S(2)}) %collective-permute-start.2) | collective-permute-done | bytes 1568 | tf_op jit(solution)/shard_map/ppermute | solution.py:14
  21.3 2.5 %collective-permute-start.3 = (f32[16,4096]{1,0:T(8,128)S(1)}, f32[16,4096]{1,0:T(8,128)S(1)}, u32[]{:S(2)}, u32[]{:S(2)}) collective-permute-start(f32[16,4096]{1,0:T(8,128)S(1)} %fusion.16), channel_id=1, source_target_pairs={{0,4},{2,6},{4,0},{6,2},{8,12},{10,14},{12,8},{14,10},{1,5},{3,7},... | collective-permute-start | bytes 786440 | tf_op jit(solution)/shard_map/ppermute | solution.py:18
  23.8 6.6 %collective-permute-done.3 = f32[16,4096]{1,0:T(8,128)S(1)} collective-permute-done((f32[16,4096]{1,0:T(8,128)S(1)}, f32[16,4096]{1,0:T(8,128)S(1)}, u32[]{:S(2)}, u32[]{:S(2)}) %collective-permute-start.3) | collective-permute-done | bytes 262176 | tf_op jit(solution)/shard_map/ppermute | solution.py:18
  30.5 1.3 collective-permute-start.4
  31.8 1.7 %collective-permute-done.4 = f32[16,48]{1,0:T(8,128)S(1)} collective-permute-done((f32[16,48]{1,0:T(8,128)S(1)}, f32[16,48]{1,0:T(8,128)S(1)}, u32[]{:S(2)}, u32[]{:S(2)}) %collective-permute-start.4) | collective-permute-done | bytes 3104 | tf_op jit(solution)/shard_map/ppermute | solution.py:14
  34.5 2.8 %collective-permute-start.5 = (f32[16,4096]{1,0:T(8,128)S(1)}, f32[16,4096]{1,0:T(8,128)S(1)}, u32[]{:S(2)}, u32[]{:S(2)}) collective-permute-start(f32[16,4096]{1,0:T(8,128)S(1)} %fusion.15), channel_id=1, source_target_pairs={{0,8},{2,10},{4,12},{6,14},{8,0},{10,2},{12,4},{14,6},{1,9},{3,11}... | collective-permute-start | bytes 786440 | tf_op jit(solution)/shard_map/ppermute | solution.py:18
  37.5 54.4 %gather_fusion.1 = f32[16384,8]{1,0:T(8,128)} fusion(f32[8,128]{0,1:T(8,128)S(1)} %copy.23, s32[16384]{0:T(1024)S(1)} %bitcast_clamp_fusion), kind=kCustom, calls=%fused_computation.1.clone | custom fusion | bytes 1114112 | tf_op jit(solution)/shard_map/jit(_take)/gather | solution.py:59
  91.9 5.1 %copy.26 = f32[128,128,8]{1,0,2:T(8,128)S(1)} copy(f32[128,128,8]{2,1,0:T(8,128)} %bitcast.161) | data formatting | bytes 1048576 | tf_op jit(solution)/shard_map/jit(_take)/gather | solution.py:59
  97.2 1.3 collective-permute-start.6
  98.5 54.4 %gather_fusion = f32[16384,8]{1,0:T(8,128)} fusion(f32[8,128]{0,1:T(8,128)S(1)} %copy.23, s32[16384]{0:T(1024)S(1)} %bitcast_clamp_fusion.1), kind=kCustom, calls=%fused_computation.clone | custom fusion | bytes 1114112 | tf_op jit(solution)/shard_map/jit(_take)/gather | solution.py:54
  152.9 5.1 %copy.24 = f32[128,128,8]{1,0,2:T(8,128)S(1)} copy(f32[128,128,8]{2,1,0:T(8,128)} %bitcast.160) | data formatting | bytes 1048576 | tf_op jit(solution)/shard_map/jit(_take)/gather | solution.py:54
  159.2 1.5 collective-permute-start.7
  160.8 1.5 collective-permute-done.7
  162.8 0.4 fusion.21
  163.2 0.4 fusion.22
  163.5 0.4 fusion.23
  164.3 0.4 fusion.25
  164.7 0.4 fusion.26
  165.4 0.4 fusion
  166.1 0.4 fusion.1
  166.7 0.4 fusion.2
  167.4 0.4 fusion.3
  169.4 0.4 fusion.6
  170.1 0.4 fusion.7
  170.8 0.6 broadcast_multiply_fusion
  (123 shorter events, 11.3 us)
Async XLA Ops:
  0.0 2.0 %copy-start = (s32[6,128]{1,0:T(8,128)S(1)}, s32[6,128]{1,0:T(8,128)}, u32[]{:S(2)}) copy-start(s32[6,128]{1,0:T(8,128)} %param.8) | copy-start | bytes 9220
  0.7 3.0 %collective-permute-start = (f32[8,36]{1,0:T(8,128)S(1)}, f32[8,36]{1,0:T(8,128)S(1)}, u32[]{:S(2)}, u32[]{:S(2)}) collective-permute-start(f32[8,36]{1,0:T(8,128)S(1)} %slice.299), channel_id=1, source_target_pairs={{1,0},{3,2},{5,4},{7,6},{9,8},{11,10},{13,12},{15,14},{17,16},{19,... | collective-permute-start | bytes 3464 | tf_op jit(solution)/shard_map/ppermute | solution.py:14
  7.0 30.4 %copy-start.1 = (f32[8,128]{1,0:T(8,128)S(1)}, f32[8,128]{1,0:T(8,128)}, u32[]{:S(2)}) copy-start(f32[8,128]{1,0:T(8,128)} %param.9) | copy-start | bytes 12292
  7.6 9.8 %collective-permute-start.1 = (f32[16,4096]{1,0:T(8,128)S(1)}, f32[16,4096]{1,0:T(8,128)S(1)}, u32[]{:S(2)}, u32[]{:S(2)}) collective-permute-start(f32[16,4096]{1,0:T(8,128)S(1)} %fusion.19), channel_id=1, source_target_pairs={{0,2},{2,0},{4,6},{6,4},{8,10},{10,8},{12,14},{14,12},{1,3},{3,1},... | collective-permute-start | bytes 786440 | tf_op jit(solution)/shard_map/ppermute | solution.py:18
  17.5 3.1 %collective-permute-start.2 = (f32[16,24]{1,0:T(8,128)S(1)}, f32[16,24]{1,0:T(8,128)S(1)}, u32[]{:S(2)}, u32[]{:S(2)}) collective-permute-start(f32[16,24]{1,0:T(8,128)S(1)} %slice.428), channel_id=1, source_target_pairs={{1,0},{3,2},{5,4},{7,6},{9,8},{11,10},{13,12},{15,14},{17,16},{19,... | collective-permute-start | bytes 4616 | tf_op jit(solution)/shard_map/ppermute | solution.py:14
  21.3 9.1 %collective-permute-start.3 = (f32[16,4096]{1,0:T(8,128)S(1)}, f32[16,4096]{1,0:T(8,128)S(1)}, u32[]{:S(2)}, u32[]{:S(2)}) collective-permute-start(f32[16,4096]{1,0:T(8,128)S(1)} %fusion.16), channel_id=1, source_target_pairs={{0,4},{2,6},{4,0},{6,2},{8,12},{10,14},{12,8},{14,10},{1,5},{3,7},... | collective-permute-start | bytes 786440 | tf_op jit(solution)/shard_map/ppermute | solution.py:18
  30.5 3.1 %collective-permute-start.4 = (f32[16,48]{1,0:T(8,128)S(1)}, f32[16,48]{1,0:T(8,128)S(1)}, u32[]{:S(2)}, u32[]{:S(2)}) collective-permute-start(f32[16,48]{1,0:T(8,128)S(1)} %slice.438), channel_id=1, source_target_pairs={{1,0},{3,2},{5,4},{7,6},{9,8},{11,10},{13,12},{15,14},{17,16},{19,... | collective-permute-start | bytes 9224 | tf_op jit(solution)/shard_map/ppermute | solution.py:14
  34.5 62.6 %collective-permute-start.5 = (f32[16,4096]{1,0:T(8,128)S(1)}, f32[16,4096]{1,0:T(8,128)S(1)}, u32[]{:S(2)}, u32[]{:S(2)}) collective-permute-start(f32[16,4096]{1,0:T(8,128)S(1)} %fusion.15), channel_id=1, source_target_pairs={{0,8},{2,10},{4,12},{6,14},{8,0},{10,2},{12,4},{14,6},{1,9},{3,11}... | collective-permute-start | bytes 786440 | tf_op jit(solution)/shard_map/ppermute | solution.py:18
  97.2 60.9 %collective-permute-start.6 = (f32[16,96]{1,0:T(8,128)S(1)}, f32[16,96]{1,0:T(8,128)S(1)}, u32[]{:S(2)}, u32[]{:S(2)}) collective-permute-start(f32[16,96]{1,0:T(8,128)S(1)} %slice.450), channel_id=1, source_target_pairs={{1,0},{3,2},{5,4},{7,6},{9,8},{11,10},{13,12},{15,14},{17,16},{19,... | collective-permute-start | bytes 18440 | tf_op jit(solution)/shard_map/ppermute | solution.py:14
  159.2 3.1 %collective-permute-start.7 = (f32[16,127]{1,0:T(8,128)S(1)}, f32[16,127]{1,0:T(8,128)S(1)}, u32[]{:S(2)}, u32[]{:S(2)}) collective-permute-start(f32[16,127]{1,0:T(8,128)S(1)} %slice.465), channel_id=1, source_target_pairs={{1,0},{3,2},{5,4},{7,6},{9,8},{11,10},{13,12},{15,14},{17,16},{19,... | collective-permute-start | bytes 24392 | tf_op jit(solution)/shard_map/ppermute | solution.py:14
where the time goes:
time: 172 us; the launch traced here: 171 us
  local copies, waits for them, and re-layouts  123 us (72%)
  waiting for transfers between devices  18.5 us (11%)
  starting transfers between devices  14.9 us (9%)
  other arithmetic  8.16 us (5%)
  matrix products  5.81 us (3%)
    gather x2, local copies, waits for them, and re-layouts, toeplitz_pair(): jnp.take(filter_bank, jnp.clip(lag_index, 0, tap_count - 1), axis=1)  59.6 us
    gather x2, local copies, waits for them, and re-layouts, toeplitz_pair(): jnp.take(filter_bank, jnp.clip(lag_later, 0, tap_count - 1), axis=1)  59.6 us
    ppermute x3, waiting for transfers between devices, from_partner(): lax.ppermute(array, axis, [(i, i ^ 1 << distance) for i in range(lax.axis...  13.4 us
    ppermute x3, starting transfers between devices, from_partner(): lax.ppermute(array, axis, [(i, i ^ 1 << distance) for i in range(lax.axis...  8.27 us
    ppermute x5, starting transfers between devices, from_behind(): return lax.ppermute(block, axis, route)  6.63 us
    ppermute x5, waiting for transfers between devices, from_behind(): return lax.ppermute(block, axis, route)  5.07 us
    select_n x26, other arithmetic, shifted_rows(): jnp.where(chosen, current[:, step:], current[:, :current.shape[1] - step])  3.54 us
  transfers between devices with their start and end apart: 8, of which 6 were waited for; matrix products, arithmetic and copies ran while one was open for 71% of the time, Pallas kernels for 0%

commit v1 on v0

--- a/solution.py
+++ b/solution.py
@@ -1,6 +1,10 @@
+import functools
+
 import jax
 import jax.numpy as jnp
 from jax import lax
+from jax.experimental import pallas as pl
+from jax.experimental.pallas import tpu as pltpu
 from jax.sharding import PartitionSpec as P
 
 SHIFT_UNIT = 3
@@ -133,7 +137,372 @@
     return jnp.stack(outputs, axis=1) / (BLOCK * channels)
 
 
+LANES = 128
+GROUP = 8
+TILES = 8
+MESH = pl.DeviceIdType.MESH
+
+
+def butterfly_partner(place, mask):
+    partner = place
+    for bit in range(3):
+        if mask >> bit & 1:
+            own = (place // 2**bit) % 2
+            partner = partner + (1 - 2 * own) * 2**bit
+    return partner
+
+
+def advanced(row, following, amount, lane):
+    picked = jnp.where(lane < amount, following, row)
+    return pltpu.roll(picked, (LANES - amount) % LANES, 1)
+
+
+def next_sublane(row):
+    return pltpu.roll(row, TILES - 1, 0)
+
+
+def butterflies(rows, shift_of, lane):
+    for section in range(3):
+        gap = 2**section
+        merged = list(rows)
+        for low in range(8):
+            if low & gap:
+                continue
+            up = rows[low + gap]
+            following = next_sublane(up)
+            merged[low] = rows[low] + advanced(up, following, shift_of(section, low), lane)
+            merged[low + gap] = rows[low] + advanced(
+                up, following, shift_of(section, low + gap), lane
+            )
+        rows = merged
+    return rows
+
+
+def split(values):
+    high = values.astype(jnp.bfloat16)
+    low = (values - high.astype(jnp.float32)).astype(jnp.bfloat16)
+    return high, low
+
+
+def kernel(
+    own_tiles,
+    window,
+    chan_shift,
+    sec_shift,
+    bank,
+    samples_in,
+    out,
+    arrived,
+    series,
+    weight_high,
+    weight_low,
+    energies,
+    local_sem,
+    send_sem,
+    recv_sem,
+    rim_send_sem,
+    rim_recv_sem,
+    out_send_sem,
+    out_recv_sem,
+):
+    me = lax.axis_index("freq")
+    half = lax.axis_index("tm")
+    last = GROUP - 1
+    own_rows = own_tiles * 8
+    window_rows = window * 8
+    rim_rows = window_rows - own_rows
+    is_last = me == last
+    lane = lax.broadcasted_iota(jnp.int32, (TILES, LANES), 1)
+
+    barrier = pltpu.get_barrier_semaphore()
+    for mask in range(1, GROUP):
+        pl.semaphore_signal(
+            barrier, inc=1, device_id={"freq": butterfly_partner(me, mask)}, device_id_type=MESH
+        )
+
+    @pl.when(jnp.logical_and(is_last, half == 0))
+    def _():
+        for place in range(GROUP):
+            pl.semaphore_signal(
+                barrier, inc=1, device_id={"freq": place, "tm": 1}, device_id_type=MESH
+            )
+
+    def own_copy(rows):
+        return pltpu.make_async_copy(
+            samples_in.at[pl.ds(me * own_rows, rows), :],
+            arrived.at[me, pl.ds(0, rows), :],
+            local_sem,
+        )
+
+    def sent(target, rows):
+        return pltpu.make_async_remote_copy(
+            src_ref=samples_in.at[pl.ds(target * own_rows, rows), :],
+            dst_ref=arrived.at[me, pl.ds(0, rows), :],
+            send_sem=send_sem.at[target],
+            recv_sem=recv_sem.at[me],
+            device_id={"freq": target},
+            device_id_type=MESH,
+        )
+
+    def awaited(source, rows):
+        return pltpu.make_async_remote_copy(
+            src_ref=samples_in.at[pl.ds(0, rows), :],
+            dst_ref=arrived.at[source, pl.ds(0, rows), :],
+            send_sem=send_sem.at[source],
+            recv_sem=recv_sem.at[source],
+            device_id={"freq": source},
+            device_id_type=MESH,
+        )
+
+    def rim():
+        return pltpu.make_async_remote_copy(
+            src_ref=samples_in.at[pl.ds(0, rim_rows), :],
+            dst_ref=arrived.at[me, pl.ds(own_rows, rim_rows), :],
+            send_sem=rim_send_sem,
+            recv_sem=rim_recv_sem.at[me],
+            device_id={"freq": last, "tm": 0},
+            device_id_type=MESH,
+        )
+
+    def rim_awaited(source):
+        return pltpu.make_async_remote_copy(
+            src_ref=samples_in.at[pl.ds(0, rim_rows), :],
+            dst_ref=arrived.at[source, pl.ds(own_rows, rim_rows), :],
+            send_sem=rim_send_sem,
+            recv_sem=rim_recv_sem.at[source],
+            device_id={"freq": last, "tm": 1},
+            device_id_type=MESH,
+        )
+
+    @pl.when(is_last)
+    def _():
+        own_copy(own_rows).start()
+
+    @pl.when(jnp.logical_not(is_last))
+    def _():
+        own_copy(window_rows).start()
+
+    for source in range(GROUP):
+        arrived[source, window_rows:, :] = jnp.zeros((TILES * 8 - window_rows, LANES), jnp.float32)
+
+    @pl.when(jnp.logical_and(is_last, half == 1))
+    def _():
+        for source in range(GROUP):
+            arrived[source, own_rows:window_rows, :] = jnp.zeros((rim_rows, LANES), jnp.float32)
+
+    pl.semaphore_wait(barrier, GROUP - 1 + half)
+
+    for mask in (6, 7, 4, 5, 2, 3, 1):
+        target = butterfly_partner(me, mask)
+
+        @pl.when(target == last)
+        def _():
+            sent(target, own_rows).start()
+
+        @pl.when(target != last)
+        def _():
+            sent(target, window_rows).start()
+
+    @pl.when(half == 1)
+    def _():
+        rim().start()
+
+    padded = jnp.concatenate([bank[...], jnp.zeros_like(bank[...])], axis=1)
+    filters = padded.shape[0]
+    for index in range(filters):
+        spread = jnp.broadcast_to(padded[index : index + 1], (LANES, 2 * LANES))
+        band = pltpu.roll(spread, 0, 1, stride=1, stride_axis=0)
+        high, low = split(band)
+        weight_high[pl.ds(index * LANES, LANES), :] = high
+        weight_low[pl.ds(index * LANES, LANES), :] = low
+
+    def take_source(source):
+        @pl.loop(0, 2)
+        def _(trial):
+            rows = []
+            for channel in range(8):
+                raw = arrived[source, pl.ds(channel, TILES, stride=8), :]
+                amount = chan_shift[trial, source * 8 + channel]
+                rows.append(advanced(raw, next_sublane(raw), amount, lane))
+            rows = butterflies(
+                rows, lambda s, p: sec_shift[s, source * 16 + p * 2 + trial], lane
+            )
+            for position in range(8):
+                start = pl.multiple_of((source * 16 + position * 2 + trial) * TILES, TILES)
+                series[pl.ds(start, TILES), :] = rows[position]
+
+    @pl.when(is_last)
+    def _():
+        own_copy(own_rows).wait()
+
+    @pl.when(jnp.logical_not(is_last))
+    def _():
+        own_copy(window_rows).wait()
+
+    for mask in (0, 1, 2, 3, 4, 5, 6, 7):
+        source = butterfly_partner(me, mask)
+        if mask:
+
+            @pl.when(is_last)
+            def _():
+                awaited(source, own_rows).wait_recv()
+
+            @pl.when(jnp.logical_not(is_last))
+            def _():
+                awaited(source, window_rows).wait_recv()
+
+        @pl.when(jnp.logical_and(is_last, half == 0))
+        def _():
+            rim_awaited(source).wait_recv()
+
+        take_source(source)
+
+    @pl.loop(0, 16)
+    def _(row):
+        places = [pl.multiple_of((row + 16 * p) * TILES, TILES) for p in range(8)]
+        rows = [series[pl.ds(place, TILES), :] for place in places]
+        rows = butterflies(rows, lambda s, p: sec_shift[s + 3, row + 16 * p], lane)
+        for place, values in zip(places, rows):
+            series[pl.ds(place, TILES), :] = values
+
+    tiles = [split(series[pl.ds(tile, LANES, stride=TILES), :]) for tile in range(own_tiles + 1)]
+    inputs = [
+        jnp.concatenate(
+            [
+                jnp.concatenate([tiles[tile][part], tiles[tile + 1][part]], axis=1)
+                for tile in range(own_tiles)
+            ],
+            axis=0,
+        )
+        for part in range(2)
+    ]
+
+    def product(left, right):
+        return lax.dot_general(
+            left, right, (((1,), (1,)), ((), ())), preferred_element_type=jnp.float32
+        )
+
+    sums = []
+    for index in range(filters):
+        high = weight_high[pl.ds(index * LANES, LANES), :]
+        low = weight_low[pl.ds(index * LANES, LANES), :]
+        filtered = product(high, inputs[0]) + product(high, inputs[1]) + product(low, inputs[0])
+        energy = jnp.sum(filtered * filtered, axis=0, keepdims=True)
+        total = energy[:, :LANES]
+        for tile in range(1, own_tiles):
+            total = total + energy[:, tile * LANES : (tile + 1) * LANES]
+        sums.append(total)
+    energies[me] = jnp.concatenate(sums, axis=0)
+
+    def energy_copy(target, place):
+        return pltpu.make_async_remote_copy(
+            src_ref=energies.at[me],
+            dst_ref=energies.at[place],
+            send_sem=out_send_sem.at[target],
+            recv_sem=out_recv_sem.at[place],
+            device_id={"freq": target},
+            device_id_type=MESH,
+        )
+
+    for mask in (6, 7, 4, 5, 2, 3, 1):
+        energy_copy(butterfly_partner(me, mask), me).start()
+    for mask in (1, 2, 3, 4, 5, 6, 7):
+        partner = butterfly_partner(me, mask)
+        energy_copy(partner, partner).wait_recv()
+    turn = ((GROUP - me) % GROUP) * 16
+    per_block = GROUP // out.shape[1]
+    for block in range(out.shape[1]):
+        total = energies[block * per_block]
+        for place in range(block * per_block + 1, (block + 1) * per_block):
+            total = total + energies[place]
+        total = pltpu.roll(total, turn, 1) * (1.0 / (BLOCK * GROUP * 8))
+        for index in range(filters):
+            out[index, block : block + 1, :] = total[index : index + 1, : out.shape[2]]
+
+    for mask in range(1, GROUP):
+        target = butterfly_partner(me, mask)
+
+        @pl.when(target == last)
+        def _():
+            sent(target, own_rows).wait_send()
+
+        @pl.when(target != last)
+        def _():
+            sent(target, window_rows).wait_send()
+
+        energy_copy(target, me).wait_send()
+
+    @pl.when(half == 1)
+    def _():
+        rim().wait_send()
+
+
+def fused_body(intensity, channel_shift, section_shift, filter_bank):
+    chan_dev, samples = intensity.shape
+    tile_count = samples // LANES
+    own_tiles = tile_count // GROUP
+    reach = CHAN_MAX + SHIFT_UNIT * (2 ** section_shift.shape[0] - 1) + LANES
+    window = own_tiles + -(-reach // LANES)
+    filters = filter_bank.shape[0]
+    blocks = samples // BLOCK
+    by_tile = intensity.reshape(chan_dev, tile_count, LANES).transpose(1, 0, 2)
+    by_tile = by_tile.reshape(tile_count * chan_dev, LANES)
+    smem = pl.BlockSpec(memory_space=pltpu.SMEM)
+    vmem = pl.BlockSpec(memory_space=pltpu.VMEM)
+    dma = pltpu.SemaphoreType.DMA
+    maps = pl.pallas_call(
+        functools.partial(kernel, own_tiles, window),
+        out_shape=jax.ShapeDtypeStruct((filters, blocks, LANES // GROUP), jnp.float32),
+        in_specs=[smem, smem, vmem, pl.BlockSpec(memory_space=pl.ANY)],
+        out_specs=vmem,
+        scratch_shapes=[
+            pltpu.VMEM((GROUP, TILES * chan_dev, LANES), jnp.float32),
+            pltpu.VMEM((LANES * TILES, LANES), jnp.float32),
+            pltpu.VMEM((filters * LANES, 2 * LANES), jnp.bfloat16),
+            pltpu.VMEM((filters * LANES, 2 * LANES), jnp.bfloat16),
+            pltpu.VMEM((GROUP, filters, LANES), jnp.float32),
+            dma,
+            dma((GROUP,)),
+            dma((GROUP,)),
+            dma,
+            dma((GROUP,)),
+            dma((GROUP,)),
+            dma((GROUP,)),
+        ],
+        compiler_params=pltpu.CompilerParams(
+            collective_id=0, has_side_effects=True, vmem_limit_bytes=32 * 2**20
+        ),
+    )(channel_shift.T, section_shift, filter_bank, by_tile)
+    return maps.transpose(2, 0, 1)
+
+
+def fits_fused(mesh, intensity, channel_shift, section_shift, filter_bank):
+    groups, halves = mesh.shape["freq"], mesh.shape["tm"]
+    samples = intensity.shape[1] // halves
+    channels, trials_each = channel_shift.shape
+    own = samples // groups
+    reach = CHAN_MAX + SHIFT_UNIT * (2 ** section_shift.shape[0] - 1) + LANES
+    return (
+        groups == GROUP
+        and halves == 2
+        and channels == 8 * GROUP
+        and trials_each == 2
+        and filter_bank.shape == (8, LANES)
+        and own % LANES == 0
+        and BLOCK % own == 0
+        and reach <= own
+        and own + reach <= (TILES - 1) * LANES
+    )
+
+
 def solution(mesh):
     in_specs = (P(("beam", "freq"), "tm"), P(), P(), P())
     out_specs = P(("beam", "freq"), None, "tm")
-    return jax.shard_map(body, mesh=mesh, in_specs=in_specs, out_specs=out_specs, check_vma=False)
+
+    def whole(*arrays):
+        chosen = fused_body if fits_fused(mesh, *arrays) else body
+        return jax.shard_map(
+            chosen, mesh=mesh, in_specs=in_specs, out_specs=out_specs, check_vma=False
+        )(*arrays)
+
+    return whole

time: 172 us -> 29.6 us (0.17)
  local copies, waits for them, and re-layouts: 123 us -> 3.56 us
  Pallas kernels: 0 us -> 25.8 us
  waiting for transfers between devices: 18.5 us -> 0 us
  starting transfers between devices: 14.9 us -> 0 us
  other arithmetic: 8.16 us -> 0 us
  matrix products: 5.81 us -> 0 us
    gather x4 -> x0, local copies, waits for them, and re-layouts: 119 us -> none  [the longest x2 59.6 us: toeplitz_pair(): jnp.take(filter_bank, jnp.clip(lag_index, 0, tap_count - 1), axis=1)]
    pallas_call x0 -> x1, Pallas kernels: none -> 25.8 us  [fused_body(): pl.pallas_call(functools.partial(kernel, own_tiles, window), out_shape=ja...]
    ppermute x8 -> x0, waiting for transfers between devices: 18.5 us -> none  [the longest x3 13.4 us: from_partner(): lax.ppermute(array, axis, [(i, i ^ 1 << distance) for i in range(lax.axis...]
    ppermute x8 -> x0, starting transfers between devices: 14.9 us -> none  [the longest x3 8.27 us: from_partner(): lax.ppermute(array, axis, [(i, i ^ 1 << distance) for i in range(lax.axis...]
    dot_general x16 -> x0, matrix products: 5.81 us -> none  [the longest x8 2.92 us: body(): jnp.dot(first_half, toep_top[filter_index], precision=lax.Precision.HIGHE...]
    select_n x31 -> x0, other arithmetic: 3.74 us -> none  [the longest x26 3.54 us: shifted_rows(): jnp.where(chosen, current[:, step:], current[:, :current.shape[1] - step])]
    unnamed x12 -> x9, local copies, waits for them, and re-layouts: 0.16 us -> 3.56 us
  transfers between devices with their start and end apart: 8 -> 0, of which waited for: 6 -> 0; matrix products, arithmetic and copies ran while one was open for 71% -> 0% of each run, Pallas kernels for 0% -> 0%
where the time goes in v1:
time: 29.6 us; the launch traced here: 29.4 us
  Pallas kernels  25.8 us (87%)
  local copies, waits for them, and re-layouts  3.56 us (12%)
    pallas_call x1, Pallas kernels, fused_body(): pl.pallas_call(functools.partial(kernel, own_tiles, window), out_shape=ja...  25.8 us
    unnamed x9, local copies, waits for them, and re-layouts  3.56 us

profile of v1, /device:TPU:0, one launch (start us, length us, event | category | flops | bytes accessed | tf_op | source)
XLA Modules:
  0.0 29.4 jit_solution(5410081905990132113)
XLA Ops:
  0.0 0.0 copy-start.3
  0.0 0.7 %copy-done.3 = s32[64,2]{0,1:T(2,128)S(1)} copy-done((s32[64,2]{0,1:T(2,128)S(1)}, s32[64,2]{0,1:T(2,128)}, u32[]{:S(2)}) %copy-start.3) | copy-done | bytes 536
  0.7 0.0 copy-start
  0.7 0.9 %copy-done = f32[8,4096]{1,0:T(8,128)S(1)} copy-done((f32[8,4096]{1,0:T(8,128)S(1)}, f32[8,4096]{1,0:T(8,128)}, u32[]{:S(2)}) %copy-start) | copy-done | bytes 131096
  1.6 0.0 copy-start.1
  1.6 0.7 %copy-done.1 = s32[6,128]{1,0:T(8,128)S(1)} copy-done((s32[6,128]{1,0:T(8,128)S(1)}, s32[6,128]{1,0:T(8,128)}, u32[]{:S(2)}) %copy-start.1) | copy-done | bytes 3096
  2.3 0.0 copy-start.2
  2.3 0.7 %copy-done.2 = f32[8,128]{1,0:T(8,128)S(1)} copy-done((f32[8,128]{1,0:T(8,128)S(1)}, f32[8,128]{1,0:T(8,128)}, u32[]{:S(2)}) %copy-start.2) | copy-done | bytes 4120
  3.0 25.8 %shard_map.46 = f32[8,4,16]{2,1,0:T(4,128)S(1)} custom-call(s32[2,64]{1,0:T(2,128)S(1)} %bitcast.9, s32[6,128]{1,0:T(8,128)S(1)} %copy-done.1, f32[8,128]{1,0:T(8,128)S(1)} %copy-done.2, f32[256,128]{1,0:T(8,128)S(1)} %bitcast.7), custom_call_target="tpu_custom_call" | custom-call | tf_op jit(solution)/shard_map/pallas_call | solution.py:453
  28.7 0.6 %copy.6 = f32[16,8,4]{0,2,1:T(4,128)} copy(f32[16,8,4]{0,2,1:T(4,128)S(1)} %bitcast.8) | data formatting | bytes 4096
Async XLA Ops:
  0.0 0.7 %copy-start.3 = (s32[64,2]{0,1:T(2,128)S(1)}, s32[64,2]{0,1:T(2,128)}, u32[]{:S(2)}) copy-start(s32[64,2]{0,1:T(2,128)} %param.5) | copy-start | bytes 1540
  0.7 0.9 %copy-start = (f32[8,4096]{1,0:T(8,128)S(1)}, f32[8,4096]{1,0:T(8,128)}, u32[]{:S(2)}) copy-start(f32[8,4096]{1,0:T(8,128)} %param.4) | copy-start | bytes 393220
  1.6 0.7 %copy-start.1 = (s32[6,128]{1,0:T(8,128)S(1)}, s32[6,128]{1,0:T(8,128)}, u32[]{:S(2)}) copy-start(s32[6,128]{1,0:T(8,128)} %sec_shift.1) | copy-start | bytes 9220
  2.3 0.7 %copy-start.2 = (f32[8,128]{1,0:T(8,128)S(1)}, f32[8,128]{1,0:T(8,128)}, u32[]{:S(2)}) copy-start(f32[8,128]{1,0:T(8,128)} %bank.1) | copy-start | bytes 12292

commit v2 on v1

--- a/solution.py
+++ b/solution.py
@@ -187,16 +187,19 @@
 def kernel(
     own_tiles,
     window,
+    chan_shift_in,
+    sec_shift_in,
+    bank_in,
+    samples_in,
+    out,
     chan_shift,
     sec_shift,
     bank,
-    samples_in,
-    out,
     arrived,
     series,
-    weight_high,
-    weight_low,
+    weights,
     energies,
+    table_sem,
     local_sem,
     send_sem,
     recv_sem,
@@ -220,6 +223,15 @@
             barrier, inc=1, device_id={"freq": butterfly_partner(me, mask)}, device_id_type=MESH
         )
 
+    tables = [
+        pltpu.make_async_copy(source, held, table_sem.at[index])
+        for index, (source, held) in enumerate(
+            ((bank_in, bank), (chan_shift_in, chan_shift), (sec_shift_in, sec_shift))
+        )
+    ]
+    for table in tables:
+        table.start()
+
     @pl.when(jnp.logical_and(is_last, half == 0))
     def _():
         for place in range(GROUP):
@@ -307,18 +319,18 @@
     def _():
         rim().start()
 
+    for table in tables:
+        table.wait()
     padded = jnp.concatenate([bank[...], jnp.zeros_like(bank[...])], axis=1)
     filters = padded.shape[0]
     for index in range(filters):
         spread = jnp.broadcast_to(padded[index : index + 1], (LANES, 2 * LANES))
         band = pltpu.roll(spread, 0, 1, stride=1, stride_axis=0)
         high, low = split(band)
-        weight_high[pl.ds(index * LANES, LANES), :] = high
-        weight_low[pl.ds(index * LANES, LANES), :] = low
+        weights[pl.ds(index * LANES, LANES), :] = jnp.concatenate([high, high, low], axis=1)
 
     def take_source(source):
-        @pl.loop(0, 2)
-        def _(trial):
+        for trial in range(2):
             rows = []
             for channel in range(8):
                 raw = arrived[source, pl.ds(channel, TILES, stride=8), :]
@@ -357,7 +369,7 @@
 
         take_source(source)
 
-    @pl.loop(0, 16)
+    @pl.loop(0, 16, unroll=4)
     def _(row):
         places = [pl.multiple_of((row + 16 * p) * TILES, TILES) for p in range(8)]
         rows = [series[pl.ds(place, TILES), :] for place in places]
@@ -366,32 +378,26 @@
             series[pl.ds(place, TILES), :] = values
 
     tiles = [split(series[pl.ds(tile, LANES, stride=TILES), :]) for tile in range(own_tiles + 1)]
-    inputs = [
-        jnp.concatenate(
-            [
-                jnp.concatenate([tiles[tile][part], tiles[tile + 1][part]], axis=1)
-                for tile in range(own_tiles)
-            ],
-            axis=0,
-        )
-        for part in range(2)
-    ]
-
-    def product(left, right):
-        return lax.dot_general(
-            left, right, (((1,), (1,)), ((), ())), preferred_element_type=jnp.float32
-        )
-
+    inputs = jnp.concatenate(
+        [
+            jnp.concatenate(
+                [tiles[tile + step][part] for part in (0, 1, 0) for step in range(2)], axis=1
+            )
+            for tile in range(own_tiles)
+        ],
+        axis=0,
+    )
+    filtered = lax.dot_general(
+        weights[...], inputs, (((1,), (1,)), ((), ())), preferred_element_type=jnp.float32
+    )
     sums = []
     for index in range(filters):
-        high = weight_high[pl.ds(index * LANES, LANES), :]
-        low = weight_low[pl.ds(index * LANES, LANES), :]
-        filtered = product(high, inputs[0]) + product(high, inputs[1]) + product(low, inputs[0])
-        energy = jnp.sum(filtered * filtered, axis=0, keepdims=True)
-        total = energy[:, :LANES]
+        part = filtered[index * LANES : (index + 1) * LANES]
+        part = part * part
+        total = part[:, :LANES]
         for tile in range(1, own_tiles):
-            total = total + energy[:, tile * LANES : (tile + 1) * LANES]
-        sums.append(total)
+            total = total + part[:, tile * LANES : (tile + 1) * LANES]
+        sums.append(jnp.sum(total, axis=0, keepdims=True))
     energies[me] = jnp.concatenate(sums, axis=0)
 
     def energy_copy(target, place):
@@ -447,20 +453,22 @@
     blocks = samples // BLOCK
     by_tile = intensity.reshape(chan_dev, tile_count, LANES).transpose(1, 0, 2)
     by_tile = by_tile.reshape(tile_count * chan_dev, LANES)
-    smem = pl.BlockSpec(memory_space=pltpu.SMEM)
-    vmem = pl.BlockSpec(memory_space=pltpu.VMEM)
+    hbm = pl.BlockSpec(memory_space=pltpu.HBM)
     dma = pltpu.SemaphoreType.DMA
     maps = pl.pallas_call(
         functools.partial(kernel, own_tiles, window),
         out_shape=jax.ShapeDtypeStruct((filters, blocks, LANES // GROUP), jnp.float32),
-        in_specs=[smem, smem, vmem, pl.BlockSpec(memory_space=pl.ANY)],
-        out_specs=vmem,
+        in_specs=[hbm] * 4,
+        out_specs=pl.BlockSpec(memory_space=pltpu.VMEM),
         scratch_shapes=[
+            pltpu.SMEM(channel_shift.shape[::-1], jnp.int32),
+            pltpu.SMEM(section_shift.shape, jnp.int32),
+            pltpu.VMEM(filter_bank.shape, jnp.float32),
             pltpu.VMEM((GROUP, TILES * chan_dev, LANES), jnp.float32),
             pltpu.VMEM((LANES * TILES, LANES), jnp.float32),
-            pltpu.VMEM((filters * LANES, 2 * LANES), jnp.bfloat16),
-            pltpu.VMEM((filters * LANES, 2 * LANES), jnp.bfloat16),
+            pltpu.VMEM((filters * LANES, 6 * LANES), jnp.bfloat16),
             pltpu.VMEM((GROUP, filters, LANES), jnp.float32),
+            dma((3,)),
             dma,
             dma((GROUP,)),
             dma((GROUP,)),
@@ -470,7 +478,7 @@
             dma((GROUP,)),
         ],
         compiler_params=pltpu.CompilerParams(
-            collective_id=0, has_side_effects=True, vmem_limit_bytes=32 * 2**20
+            collective_id=0, has_side_effects=True, vmem_limit_bytes=60 * 2**20
         ),
     )(channel_shift.T, section_shift, filter_bank, by_tile)
     return maps.transpose(2, 0, 1)

time: 29.6 us -> 24 us (0.81)
  Pallas kernels: 25.8 us -> 22.4 us
  local copies, waits for them, and re-layouts: 3.56 us -> 1.32 us
    pallas_call x1, Pallas kernels: 25.8 us -> 22.4 us  [fused_body(): pl.pallas_call(functools.partial(kernel, own_tiles, window), out_shape=ja...]
    unnamed x9 -> x1, local copies, waits for them, and re-layouts: 3.56 us -> 1.32 us
where the time goes in v2:
time: 24 us; the launch traced here: 23.7 us
  Pallas kernels  22.4 us (93%)
  local copies, waits for them, and re-layouts  1.32 us (6%)
    pallas_call x1, Pallas kernels, fused_body(): pl.pallas_call(functools.partial(kernel, own_tiles, window), out_shape=ja...  22.4 us
    unnamed x1, local copies, waits for them, and re-layouts  1.32 us

profile of v2, /device:TPU:0, one launch (start us, length us, event | category | flops | bytes accessed | tf_op | source)
XLA Modules:
  0.0 23.7 jit_solution(15953830504098199928)
XLA Ops:
  0.0 22.4 %shard_map.46 = f32[8,4,16]{2,1,0:T(4,128)} custom-call(s32[2,64]{1,0:T(2,128)} %bitcast.9, s32[6,128]{1,0:T(8,128)} %sec_shift_in.1, f32[8,128]{1,0:T(8,128)} %bank_in.1, f32[256,128]{1,0:T(8,128)} %bitcast.7), custom_call_target="tpu_custom_call" | custom-call | tf_op jit(solution)/shard_map/pallas_call | solution.py:458
  22.4 1.3 %copy.6 = f32[16,8,4]{0,2,1:T(4,128)} copy(f32[16,8,4]{0,2,1:T(4,128)} %bitcast.8) | data formatting | bytes 4096

commit v3 on v2

--- a/solution.py
+++ b/solution.py
@@ -143,18 +143,24 @@
 MESH = pl.DeviceIdType.MESH
 
 
-def butterfly_partner(place, mask):
-    partner = place
+def butterfly_partners(place):
+    steps = []
     for bit in range(3):
-        if mask >> bit & 1:
-            own = (place // 2**bit) % 2
-            partner = partner + (1 - 2 * own) * 2**bit
-    return partner
+        own = lax.rem(lax.div(place, 2**bit), 2)
+        steps.append((1 - 2 * own) * 2**bit)
+    partners = []
+    for mask in range(GROUP):
+        partner = place
+        for bit in range(3):
+            if mask >> bit & 1:
+                partner = partner + steps[bit]
+        partners.append(partner)
+    return partners
 
 
 def advanced(row, following, amount, lane):
     picked = jnp.where(lane < amount, following, row)
-    return pltpu.roll(picked, (LANES - amount) % LANES, 1)
+    return pltpu.roll(picked, jnp.bitwise_and(LANES - amount, LANES - 1), 1)
 
 
 def next_sublane(row):
@@ -211,6 +217,7 @@
     me = lax.axis_index("freq")
     half = lax.axis_index("tm")
     last = GROUP - 1
+    partners = butterfly_partners(me)
     own_rows = own_tiles * 8
     window_rows = window * 8
     rim_rows = window_rows - own_rows
@@ -220,7 +227,7 @@
     barrier = pltpu.get_barrier_semaphore()
     for mask in range(1, GROUP):
         pl.semaphore_signal(
-            barrier, inc=1, device_id={"freq": butterfly_partner(me, mask)}, device_id_type=MESH
+            barrier, inc=1, device_id={"freq": partners[mask]}, device_id_type=MESH
         )
 
     tables = [
@@ -305,7 +312,7 @@
     pl.semaphore_wait(barrier, GROUP - 1 + half)
 
     for mask in (6, 7, 4, 5, 2, 3, 1):
-        target = butterfly_partner(me, mask)
+        target = partners[mask]
 
         @pl.when(target == last)
         def _():
@@ -330,12 +337,13 @@
         weights[pl.ds(index * LANES, LANES), :] = jnp.concatenate([high, high, low], axis=1)
 
     def take_source(source):
+        raws = [arrived[source, pl.ds(channel, TILES, stride=8), :] for channel in range(8)]
+        nexts = [next_sublane(raw) for raw in raws]
         for trial in range(2):
             rows = []
             for channel in range(8):
-                raw = arrived[source, pl.ds(channel, TILES, stride=8), :]
                 amount = chan_shift[trial, source * 8 + channel]
-                rows.append(advanced(raw, next_sublane(raw), amount, lane))
+                rows.append(advanced(raws[channel], nexts[channel], amount, lane))
             rows = butterflies(
                 rows, lambda s, p: sec_shift[s, source * 16 + p * 2 + trial], lane
             )
@@ -352,7 +360,7 @@
         own_copy(window_rows).wait()
 
     for mask in (0, 1, 2, 3, 4, 5, 6, 7):
-        source = butterfly_partner(me, mask)
+        source = partners[mask]
         if mask:
 
             @pl.when(is_last)
@@ -411,11 +419,11 @@
         )
 
     for mask in (6, 7, 4, 5, 2, 3, 1):
-        energy_copy(butterfly_partner(me, mask), me).start()
+        energy_copy(partners[mask], me).start()
     for mask in (1, 2, 3, 4, 5, 6, 7):
-        partner = butterfly_partner(me, mask)
+        partner = partners[mask]
         energy_copy(partner, partner).wait_recv()
-    turn = ((GROUP - me) % GROUP) * 16
+    turn = lax.rem(GROUP - me, GROUP) * 16
     per_block = GROUP // out.shape[1]
     for block in range(out.shape[1]):
         total = energies[block * per_block]
@@ -426,7 +434,7 @@
             out[index, block : block + 1, :] = total[index : index + 1, : out.shape[2]]
 
     for mask in range(1, GROUP):
-        target = butterfly_partner(me, mask)
+        target = partners[mask]
 
         @pl.when(target == last)
         def _():

time: 24 us -> 23.1 us (0.963)
  Pallas kernels: 22.4 us -> 21.5 us
    pallas_call x1, Pallas kernels: 22.4 us -> 21.5 us  [fused_body(): pl.pallas_call(functools.partial(kernel, own_tiles, window), out_shape=ja...]
where the time goes in v3:
time: 23.1 us; the launch traced here: 22.9 us
  Pallas kernels  21.5 us (93%)
  local copies, waits for them, and re-layouts  1.32 us (6%)
    pallas_call x1, Pallas kernels, fused_body(): pl.pallas_call(functools.partial(kernel, own_tiles, window), out_shape=ja...  21.5 us
    unnamed x1, local copies, waits for them, and re-layouts  1.32 us

profile of v3, /device:TPU:0, one launch (start us, length us, event | category | flops | bytes accessed | tf_op | source)
XLA Modules:
  0.0 22.9 jit_solution(3575891370962800188)
XLA Ops:
  0.0 21.5 %shard_map.46 = f32[8,4,16]{2,1,0:T(4,128)} custom-call(s32[2,64]{1,0:T(2,128)} %bitcast.9, s32[6,128]{1,0:T(8,128)} %sec_shift_in.1, f32[8,128]{1,0:T(8,128)} %bank_in.1, f32[256,128]{1,0:T(8,128)} %bitcast.7), custom_call_target="tpu_custom_call" | custom-call | tf_op jit(solution)/shard_map/pallas_call | solution.py:466
  21.5 1.3 %copy.6 = f32[16,8,4]{0,2,1:T(4,128)} copy(f32[16,8,4]{0,2,1:T(4,128)} %bitcast.8) | data formatting | bytes 4096

commit v4 on v3

--- a/solution.py
+++ b/solution.py
@@ -377,7 +377,7 @@
 
         take_source(source)
 
-    @pl.loop(0, 16, unroll=4)
+    @pl.loop(0, 16, unroll=8)
     def _(row):
         places = [pl.multiple_of((row + 16 * p) * TILES, TILES) for p in range(8)]
         rows = [series[pl.ds(place, TILES), :] for place in places]
@@ -386,26 +386,25 @@
             series[pl.ds(place, TILES), :] = values
 
     tiles = [split(series[pl.ds(tile, LANES, stride=TILES), :]) for tile in range(own_tiles + 1)]
-    inputs = jnp.concatenate(
-        [
-            jnp.concatenate(
-                [tiles[tile + step][part] for part in (0, 1, 0) for step in range(2)], axis=1
-            )
-            for tile in range(own_tiles)
-        ],
-        axis=0,
-    )
-    filtered = lax.dot_general(
-        weights[...], inputs, (((1,), (1,)), ((), ())), preferred_element_type=jnp.float32
-    )
-    sums = []
-    for index in range(filters):
-        part = filtered[index * LANES : (index + 1) * LANES]
-        part = part * part
-        total = part[:, :LANES]
-        for tile in range(1, own_tiles):
-            total = total + part[:, tile * LANES : (tile + 1) * LANES]
-        sums.append(jnp.sum(total, axis=0, keepdims=True))
+    sums = [None] * filters
+    for first in range(0, own_tiles, 2):
+        inputs = jnp.concatenate(
+            [
+                jnp.concatenate(
+                    [tiles[tile + step][part] for part in (0, 1, 0) for step in range(2)], axis=1
+                )
+                for tile in range(first, first + 2)
+            ],
+            axis=0,
+        )
+        filtered = lax.dot_general(
+            weights[...], inputs, (((1,), (1,)), ((), ())), preferred_element_type=jnp.float32
+        )
+        for index in range(filters):
+            part = filtered[index * LANES : (index + 1) * LANES]
+            part = part * part
+            total = jnp.sum(part[:, :LANES] + part[:, LANES:], axis=0, keepdims=True)
+            sums[index] = total if first == 0 else sums[index] + total
     energies[me] = jnp.concatenate(sums, axis=0)
 
     def energy_copy(target, place):
@@ -504,7 +503,7 @@
         and channels == 8 * GROUP
         and trials_each == 2
         and filter_bank.shape == (8, LANES)
-        and own % LANES == 0
+        and own % (2 * LANES) == 0
         and BLOCK % own == 0
         and reach <= own
         and own + reach <= (TILES - 1) * LANES

time: 23.1 us -> 22.9 us (level)
  no operation moved by 1% of the time
where the time goes in v4:
time: 22.9 us; the launch traced here: 22.6 us
  Pallas kernels  21.3 us (93%)
  local copies, waits for them, and re-layouts  1.32 us (6%)
    pallas_call x1, Pallas kernels, fused_body(): pl.pallas_call(functools.partial(kernel, own_tiles, window), out_shape=ja...  21.3 us
    unnamed x1, local copies, waits for them, and re-layouts  1.32 us

profile of v4, /device:TPU:0, one launch (start us, length us, event | category | flops | bytes accessed | tf_op | source)
XLA Modules:
  0.0 22.6 jit_solution(5780646837646352113)
XLA Ops:
  0.0 21.3 %shard_map.46 = f32[8,4,16]{2,1,0:T(4,128)} custom-call(s32[2,64]{1,0:T(2,128)} %bitcast.9, s32[6,128]{1,0:T(8,128)} %sec_shift_in.1, f32[8,128]{1,0:T(8,128)} %bank_in.1, f32[256,128]{1,0:T(8,128)} %bitcast.7), custom_call_target="tpu_custom_call" | custom-call | tf_op jit(solution)/shard_map/pallas_call | solution.py:465
  21.3 1.3 %copy.6 = f32[16,8,4]{0,2,1:T(4,128)} copy(f32[16,8,4]{0,2,1:T(4,128)} %bitcast.8) | data formatting | bytes 4096

commit v5 on v4

--- a/solution.py
+++ b/solution.py
@@ -302,7 +302,9 @@
         own_copy(window_rows).start()
 
     for source in range(GROUP):
-        arrived[source, window_rows:, :] = jnp.zeros((TILES * 8 - window_rows, LANES), jnp.float32)
+        arrived[source, window_rows:, :] = jnp.zeros(
+            (TILES * 8 + 8 - window_rows, LANES), jnp.float32
+        )
 
     @pl.when(jnp.logical_and(is_last, half == 1))
     def _():
@@ -338,7 +340,7 @@
 
     def take_source(source):
         raws = [arrived[source, pl.ds(channel, TILES, stride=8), :] for channel in range(8)]
-        nexts = [next_sublane(raw) for raw in raws]
+        nexts = [arrived[source, pl.ds(channel + 8, TILES, stride=8), :] for channel in range(8)]
         for trial in range(2):
             rows = []
             for channel in range(8):
@@ -471,7 +473,7 @@
             pltpu.SMEM(channel_shift.shape[::-1], jnp.int32),
             pltpu.SMEM(section_shift.shape, jnp.int32),
             pltpu.VMEM(filter_bank.shape, jnp.float32),
-            pltpu.VMEM((GROUP, TILES * chan_dev, LANES), jnp.float32),
+            pltpu.VMEM((GROUP, (TILES + 1) * chan_dev, LANES), jnp.float32),
             pltpu.VMEM((LANES * TILES, LANES), jnp.float32),
             pltpu.VMEM((filters * LANES, 6 * LANES), jnp.bfloat16),
             pltpu.VMEM((GROUP, filters, LANES), jnp.float32),

time: 22.9 us -> 22.9 us (level)
  no operation moved by 1% of the time
where the time goes in v5:
time: 22.9 us; the launch traced here: 22.6 us
  Pallas kernels  21.3 us (93%)
  local copies, waits for them, and re-layouts  1.32 us (6%)
    pallas_call x1, Pallas kernels, fused_body(): pl.pallas_call(functools.partial(kernel, own_tiles, window), out_shape=ja...  21.3 us
    unnamed x1, local copies, waits for them, and re-layouts  1.32 us

profile of v5, /device:TPU:0, one launch (start us, length us, event | category | flops | bytes accessed | tf_op | source)
XLA Modules:
  0.0 22.6 jit_solution(11849429046933677064)
XLA Ops:
  0.0 21.3 %shard_map.46 = f32[8,4,16]{2,1,0:T(4,128)} custom-call(s32[2,64]{1,0:T(2,128)} %bitcast.9, s32[6,128]{1,0:T(8,128)} %sec_shift_in.1, f32[8,128]{1,0:T(8,128)} %bank_in.1, f32[256,128]{1,0:T(8,128)} %bitcast.7), custom_call_target="tpu_custom_call" | custom-call | tf_op jit(solution)/shard_map/pallas_call | solution.py:467
  21.3 1.3 %copy.6 = f32[16,8,4]{0,2,1:T(4,128)} copy(f32[16,8,4]{0,2,1:T(4,128)} %bitcast.8) | data formatting | bytes 4096
